TPU v7x, 32 devices: a whole 2x2x4 slice. The times are simulated.
32 devices in a mesh: depth: 4 (over z), freq: 8 (over y, x, core).
Axes of the slice: x: 2, y: 2, z: 4, core: 2. Of those that a mesh axis runs over, the one named last changes fastest.
Arguments:
- source: float32 [8, 2, 256, 256], P('freq'), may hold values from -6 to 6
- receiver: float32 [8, 2, 256, 256], P('freq'), may hold values from -6 to 6
- classes: int32 [4, 256, 256], P('depth'), may hold values from 0 to 15
- coef_table: float32 [16, 8, 2, 6], replicated, may hold values from -2 to 2, as said below
- freq_list: int32 [8], P('freq'), may hold values from 0 to 7, each once
Outputs:
- image: float32 [256, 4, 8, 256], P('freq', 'depth')
Inputs may be any that keep to these rules, and one draw needn't show every extreme that they name: `coef_table`: every entry lies within the stated bounds.
All inputs are finite; a program needn't handle non-finite values.
Results may differ from a plain program's by a relative error of at most 0.00011.
Values sent between devices are 32-bit elements; how exact they have to be, the bound alone decides.
A program may use at most 64 MiB of HBM per device.

v0:
```python
import jax
import jax.numpy as jnp
from jax import lax
from jax.sharding import PartitionSpec as P

H = 8


def padded_2(block, sides, width):
    for axis, dim in sides:
        count = lax.axis_size(axis)
        forward = [(i, i + 1) for i in range(count - 1)]
        backward = [(target, source) for source, target in forward]
        low = lax.ppermute(
            lax.slice_in_dim(block, block.shape[dim] - width, None, axis=dim), axis, forward
        )
        high = lax.ppermute(lax.slice_in_dim(block, 0, width, axis=dim), axis, backward)
        block = jnp.concatenate([low, block, high], axis=dim)
    return block


def mcclellan(field):
    widths = [(0, 0)] * (field.ndim - 2) + [(1, 1), (1, 1)]
    padded = jnp.pad(field, widths)
    axial_sum = (
        padded[..., 2:, 1:-1]
        + padded[..., :-2, 1:-1]
        + padded[..., 1:-1, 2:]
        + padded[..., 1:-1, :-2]
    )
    corner_sum = (
        padded[..., 2:, 2:] + padded[..., 2:, :-2] + padded[..., :-2, 2:] + padded[..., :-2, :-2]
    )
    return -0.5 * field + 0.25 * axial_sum + 0.125 * corner_sum


def apply_masked(field, keep):
    moved = mcclellan(field)
    return moved * keep


def extrapolate(fields, coeffs, keep=None):
    terms = coeffs.shape[3]
    earlier = fields
    current = apply_masked(fields, keep)
    total_real = coeffs[:, :, 0, 0] * earlier[:, :, 0] - coeffs[:, :, 1, 0] * earlier[:, :, 1]
    total_imag = coeffs[:, :, 0, 0] * earlier[:, :, 1] + coeffs[:, :, 1, 0] * earlier[:, :, 0]
    for term_no in range(1, terms):
        total_real = (
            total_real
            + coeffs[:, :, 0, term_no] * current[:, :, 0]
            - coeffs[:, :, 1, term_no] * current[:, :, 1]
        )
        total_imag = (
            total_imag
            + coeffs[:, :, 0, term_no] * current[:, :, 1]
            + coeffs[:, :, 1, term_no] * current[:, :, 0]
        )
        if term_no + 1 < terms:
            following = 2.0 * apply_masked(current, keep) - earlier
            earlier, current = (current, following)
    return jnp.stack([total_real, total_imag], axis=2)


def correlate(padded_levels, row_count, offset_total, scaling):
    margin = offset_total // 2
    offsets = []
    for offset_no in range(offset_total):
        shift_x = offset_no - margin
        src_part = padded_levels[:, 0, :, :, margin - shift_x : margin - shift_x + row_count]
        rec_part = padded_levels[:, 1, :, :, margin + shift_x : margin + shift_x + row_count]
        offsets.append(jnp.sum(src_part * rec_part, axis=(1, 2)))
    stacked = jnp.stack(offsets, axis=1)
    return jnp.transpose(stacked, (2, 0, 1, 3)) * scaling


def per_device(source, receiver, classes, coef_table, freq_list):
    section = lax.axis_index("depth")
    depth_count = lax.axis_size("depth")
    freq_count = lax.axis_size("freq")
    class_count = coef_table.shape[0]
    term_count = coef_table.shape[3]
    slot_count = source.shape[0]
    rows_x = source.shape[2]
    cols_y = source.shape[3]
    offset_total = H
    margin = offset_total // 2
    scaling = float(slot_count * freq_count) ** (-0.5)
    chooser = (
        freq_list[:, None] == jnp.arange(coef_table.shape[1], dtype=jnp.int32)[None, :]
    ).astype(jnp.float32)
    local_table = jnp.einsum("fg,cgrk->frkc", chooser, coef_table, precision=lax.Precision.HIGHEST)
    imag_sign = jnp.array([1.0, -1.0], dtype=local_table.dtype)
    both_tables = jnp.stack([local_table * imag_sign[None, :, None, None], local_table])
    class_ids = jnp.arange(class_count, dtype=jnp.int32)[:, None]
    start_fields = jnp.stack([source, receiver])
    rows_here = rows_x // depth_count
    reach = term_count - 1
    first = section * rows_here
    own = lax.dynamic_slice_in_dim(start_fields, first, rows_here, 3)
    all_classes = lax.all_gather(classes, "depth", axis=0, tiled=True)
    class_padded = jnp.pad(all_classes, [(0, 0), (reach, reach), (0, 0)])
    class_block = lax.dynamic_slice_in_dim(class_padded, first, rows_here + 2 * reach, 1)
    global_row = first - reach + jnp.arange(rows_here + 2 * reach, dtype=jnp.int32)
    keep = ((global_row >= 0) & (global_row < rows_x)).astype(jnp.float32)[:, None]
    all_rows = both_tables.reshape(-1, class_count)

    def march_level(fields, class_rows):
        wide = padded_2(fields, (("depth", 3),), reach)
        one_hot = (class_rows.reshape(1, -1) == class_ids).astype(jnp.float32)
        coeffs = jnp.dot(
            all_rows, one_hot, precision=lax.Precision.HIGHEST, preferred_element_type=jnp.float32
        )
        coeffs = coeffs.reshape(2, slot_count, 2, term_count, rows_here + 2 * reach, cols_y)
        moved = extrapolate(wide, coeffs, keep)
        inner = moved[:, :, :, reach : reach + rows_here]
        return (inner, inner)

    unused, levels_all = lax.scan(march_level, own, class_block)
    wide_levels = padded_2(levels_all, (("depth", 4),), margin)
    row_terms = correlate(wide_levels, rows_here, offset_total, scaling)
    terms = lax.all_to_all(row_terms, "depth", split_axis=1, concat_axis=0, tiled=True)
    return lax.psum_scatter(terms, "freq", scatter_dimension=0, tiled=True)


def solution(mesh):
    placed = (
        P("freq", None, None, None),
        P("freq", None, None, None),
        P("depth", None, None),
        P(),
        P("freq"),
    )
    return jax.shard_map(
        per_device,
        mesh=mesh,
        in_specs=placed,
        out_specs=P("freq", "depth", None, None),
        check_vma=False,
    )
```

profile of v0, /device:TPU:26, one launch (start us, length us, event | category | flops | bytes accessed | tf_op | source)
XLA Modules:
  0.0 214.2 jit_solution(4905133129822280232)
XLA Ops:
  9.0 1.0 fusion.87
  9.9 26.5 %all-gather.2.cloned.1.call-done = s32[4,256,256]{2,1,0:T(8,128)} async-done(((s32[1,256,256]{2,1,0:T(8,128)}), s32[4,256,256]{2,1,0:T(8,128)}) %all-gather.2.cloned.1.call-update) | async-done | bytes 1048592 | tf_op jit(solution)/shard_map/all_gather | solution.py:101
  36.4 1.7 pad_dynamic-slice_fusion
  38.1 58.5 %while.15 = (s32[]{:T(128)}, f32[2,1,2,64,256]{4,3,0,2,1:T(8,128)S(1)}, f32[4,2,1,2,64,256]{5,4,1,3,2,0:T(8,128)S(1)}, s32[4,74,256]{2,1,0:T(8,128)}, f32[24,16]{0,1:T(8,128)S(1)}, /*index=5*/s32[]{:T(128)}, s32[]{:T(128)}) while((s32[]{:T(128)}, f32[2,1,2,64,256]{4,3,0,2,1:T(8,128)S(1)}, f32[4,2,1,2,64,256]{5,4,1,3,2,0:T(8,128)S(1)}, ...), condition=%wide.region_1.2_spmd.clone, body=%wide.region_0.1_spmd.clone.sunk | while | flops 95770992 | bytes 19363232 | solution.py:119
  38.1 3.4 %collective-permute-start = (f32[2,1,2,5,256]{4,3,0,2,1:T(8,128)S(1)}, f32[2,1,2,5,256]{4,3,0,2,1:T(8,128)S(1)}, u32[]{:S(2)}, u32[]{:S(2)}) collective-permute-start(f32[2,1,2,5,256]{4,3,0,2,1:T(8,128)S(1)} %get-tuple-element.190), channel_id=1, source_target_pairs={{8,0},{16,8},{24,16},{9,1},{17,9},{25,17},{10,2},{18,10},{26,18},{... | collective-permute-start | bytes 61448 | tf_op jit(solution)/shard_map/while/body/eval_jaxpr/ppermute | solution.py:17
  41.6 1.3 collective-permute-start.1
  42.9 0.9 constant_dynamic-slice_fusion.2
  43.8 2.2 %convolution_bitcast_fusion.2 = f32[24,18944]{1,0:T(8,128)} fusion(f32[24,16]{0,1:T(8,128)S(1)} %get-tuple-element.212, s32[18944]{0:T(1024)S(1)} %eq.72), kind=kOutput, calls=%fused_computation.2.clone.1 | convolution fusion | flops 87597056 | bytes 1895936 | tf_op jit(solution)/shard_map/while/body/eval_jaxpr/dot_general | solution.py:111
  45.9 1.6 reshape.453
  48.8 1.1 fusion.110
  51.9 4.5 %collective-permute-start = (f32[2,1,2,5,256]{4,3,0,2,1:T(8,128)S(1)}, f32[2,1,2,5,256]{4,3,0,2,1:T(8,128)S(1)}, u32[]{:S(2)}, u32[]{:S(2)}) collective-permute-start(f32[2,1,2,5,256]{4,3,0,2,1:T(8,128)S(1)} %get-tuple-element.190), channel_id=1, source_target_pairs={{8,0},{16,8},{24,16},{9,1},{17,9},{25,17},{10,2},{18,10},{26,18},{... | collective-permute-start | bytes 61448 | tf_op jit(solution)/shard_map/while/body/eval_jaxpr/ppermute | solution.py:17
  56.5 1.3 collective-permute-start.1
  58.7 2.2 %convolution_bitcast_fusion.2 = f32[24,18944]{1,0:T(8,128)} fusion(f32[24,16]{0,1:T(8,128)S(1)} %get-tuple-element.212, s32[18944]{0:T(1024)S(1)} %eq.72), kind=kOutput, calls=%fused_computation.2.clone.1 | convolution fusion | flops 87597056 | bytes 1895936 | tf_op jit(solution)/shard_map/while/body/eval_jaxpr/dot_general | solution.py:111
  60.8 1.6 reshape.453
  63.7 1.1 fusion.110
  66.8 4.5 %collective-permute-start = (f32[2,1,2,5,256]{4,3,0,2,1:T(8,128)S(1)}, f32[2,1,2,5,256]{4,3,0,2,1:T(8,128)S(1)}, u32[]{:S(2)}, u32[]{:S(2)}) collective-permute-start(f32[2,1,2,5,256]{4,3,0,2,1:T(8,128)S(1)} %get-tuple-element.190), channel_id=1, source_target_pairs={{8,0},{16,8},{24,16},{9,1},{17,9},{25,17},{10,2},{18,10},{26,18},{... | collective-permute-start | bytes 61448 | tf_op jit(solution)/shard_map/while/body/eval_jaxpr/ppermute | solution.py:17
  71.4 1.3 collective-permute-start.1
  72.7 0.9 constant_dynamic-slice_fusion.2
  73.6 2.2 %convolution_bitcast_fusion.2 = f32[24,18944]{1,0:T(8,128)} fusion(f32[24,16]{0,1:T(8,128)S(1)} %get-tuple-element.212, s32[18944]{0:T(1024)S(1)} %eq.72), kind=kOutput, calls=%fused_computation.2.clone.1 | convolution fusion | flops 87597056 | bytes 1895936 | tf_op jit(solution)/shard_map/while/body/eval_jaxpr/dot_general | solution.py:111
  75.7 1.6 reshape.453
  78.6 1.1 fusion.110
  81.7 4.5 %collective-permute-start = (f32[2,1,2,5,256]{4,3,0,2,1:T(8,128)S(1)}, f32[2,1,2,5,256]{4,3,0,2,1:T(8,128)S(1)}, u32[]{:S(2)}, u32[]{:S(2)}) collective-permute-start(f32[2,1,2,5,256]{4,3,0,2,1:T(8,128)S(1)} %get-tuple-element.190), channel_id=1, source_target_pairs={{8,0},{16,8},{24,16},{9,1},{17,9},{25,17},{10,2},{18,10},{26,18},{... | collective-permute-start | bytes 61448 | tf_op jit(solution)/shard_map/while/body/eval_jaxpr/ppermute | solution.py:17
  86.3 1.3 collective-permute-start.1
  88.5 2.2 %convolution_bitcast_fusion.2 = f32[24,18944]{1,0:T(8,128)} fusion(f32[24,16]{0,1:T(8,128)S(1)} %get-tuple-element.212, s32[18944]{0:T(1024)S(1)} %eq.72), kind=kOutput, calls=%fused_computation.2.clone.1 | convolution fusion | flops 87597056 | bytes 1895936 | tf_op jit(solution)/shard_map/while/body/eval_jaxpr/dot_general | solution.py:111
  90.6 1.6 reshape.453
  93.5 1.1 fusion.110
  96.6 4.6 %collective-permute-start.2 = (f32[4,2,1,2,4,256]{5,4,1,3,2,0:T(4,128)S(1)}, f32[4,2,1,2,4,256]{5,4,1,3,2,0:T(4,128)S(1)}, u32[]{:S(2)}, u32[]{:S(2)}) collective-permute-start(f32[4,2,1,2,4,256]{5,4,1,3,2,0:T(4,128)S(1)} %get-tuple-element.147), channel_id=1, source_target_pairs={{8,0},{16,8},{24,16},{9,1},{17,9},{25,17},{10,2},{18,10},{26,18},{... | collective-permute-start | bytes 196616 | tf_op jit(solution)/shard_map/ppermute | solution.py:17
  101.3 1.3 collective-permute-start.3
  103.1 4.4 %collective-permute-done.3 = f32[4,2,1,2,4,256]{5,4,1,3,2,0:T(4,128)S(1)} collective-permute-done((f32[4,2,1,2,4,256]{5,4,1,3,2,0:T(4,128)S(1)}, f32[4,2,1,2,4,256]{5,4,1,3,2,0:T(4,128)S(1)}, u32[]{:S(2)}, u32[]{:S(2)}) %collective-permute-start.3) | collective-permute-done | bytes 65568 | tf_op jit(solution)/shard_map/ppermute | solution.py:14
  112.6 5.1 %stack.67 = f32[4,8,64,256]{3,1,2,0:T(8,128)S(1)} concatenate(f32[4,1,64,256]{3,1,2,0:T(1,128)S(1)} %copy-done.1, f32[4,1,64,256]{3,1,2,0:T(1,128)S(1)} %stack.60, f32[4,1,64,256]{3,1,2,0:T(1,128)S(1)} %stack.61, f32[4,1,64,256]{3,1,2,0:T(1,128)S(1)} %stack.62, f32[4,1,64,256]{3,1,2,0:T(1,128)S(1)} %stack.63, f32[4,1,64,256]{3,1,2,0:T(1,128)} %stack.64, ...), dimensions={1} | concatenate | bytes 4194304 | tf_op jit(solution)/shard_map/stack | solution.py:73
  117.9 47.2 %all_to_all.18 = f32[64,4,8,256]{3,2,0,1:T(8,128)} all-to-all(f32[64,4,8,256]{3,2,0,1:T(8,128)S(1)} %multiply_bitcast_fusion), channel_id=1, replica_groups=mesh['depth'=4,'freq'=8] {'depth'}, dimensions={1} | all-to-all | bytes 4194304 | tf_op jit(solution)/shard_map/all_to_all | solution.py:122
  165.1 42.3 %reduce-scatter.2.cloned.1.call-done = f32[32,1,8,256]{3,2,1,0:T(8,128)} async-done(((f32[256,1,8,256]{3,2,1,0:T(8,128)}), f32[32,1,8,256]{3,2,1,0:T(8,128)}) %reduce-scatter.2.cloned.1.call-update) | async-done | bytes 262160 | tf_op jit(solution)/shard_map/reduce_scatter | solution.py:123
  (84 shorter events, 22.0 us)
Async XLA Ops:
  6.5 1.4 copy-start
  6.5 29.9 %all-gather.2.cloned.1.call-start = ((), (), s32[]{:S(2)}) async-start(), calls=%async_computation.2 | async-start | bytes 1310720 | tf_op jit(solution)/shard_map/all_gather | solution.py:101
  7.3 200.1 %reduce-scatter.2.cloned.1.call-start = ((), (), s32[]{:S(2)}) async-start(), calls=%async_computation.3 | async-start | bytes 2359296 | tf_op jit(solution)/shard_map/reduce_scatter | solution.py:123
  38.1 9.4 %collective-permute-start = (f32[2,1,2,5,256]{4,3,0,2,1:T(8,128)S(1)}, f32[2,1,2,5,256]{4,3,0,2,1:T(8,128)S(1)}, u32[]{:S(2)}, u32[]{:S(2)}) collective-permute-start(f32[2,1,2,5,256]{4,3,0,2,1:T(8,128)S(1)} %get-tuple-element.190), channel_id=1, source_target_pairs={{8,0},{16,8},{24,16},{9,1},{17,9},{25,17},{10,2},{18,10},{26,18},{... | collective-permute-start | bytes 61448 | tf_op jit(solution)/shard_map/while/body/eval_jaxpr/ppermute | solution.py:17
  41.6 6.0 %collective-permute-start.1 = (f32[2,1,2,5,256]{4,3,0,2,1:T(8,128)S(1)}, f32[2,1,2,5,256]{4,3,0,2,1:T(8,128)S(1)}, u32[]{:S(2)}, u32[]{:S(2)}) collective-permute-start(f32[2,1,2,5,256]{4,3,0,2,1:T(8,128)S(1)} %get-tuple-element.191), channel_id=1, source_target_pairs={{0,8},{8,16},{16,24},{1,9},{9,17},{17,25},{2,10},{10,18},{18,26},{... | collective-permute-start | bytes 61448 | tf_op jit(solution)/shard_map/while/body/eval_jaxpr/ppermute | solution.py:14
  51.9 10.6 %collective-permute-start = (f32[2,1,2,5,256]{4,3,0,2,1:T(8,128)S(1)}, f32[2,1,2,5,256]{4,3,0,2,1:T(8,128)S(1)}, u32[]{:S(2)}, u32[]{:S(2)}) collective-permute-start(f32[2,1,2,5,256]{4,3,0,2,1:T(8,128)S(1)} %get-tuple-element.190), channel_id=1, source_target_pairs={{8,0},{16,8},{24,16},{9,1},{17,9},{25,17},{10,2},{18,10},{26,18},{... | collective-permute-start | bytes 61448 | tf_op jit(solution)/shard_map/while/body/eval_jaxpr/ppermute | solution.py:17
  56.5 6.0 %collective-permute-start.1 = (f32[2,1,2,5,256]{4,3,0,2,1:T(8,128)S(1)}, f32[2,1,2,5,256]{4,3,0,2,1:T(8,128)S(1)}, u32[]{:S(2)}, u32[]{:S(2)}) collective-permute-start(f32[2,1,2,5,256]{4,3,0,2,1:T(8,128)S(1)} %get-tuple-element.191), channel_id=1, source_target_pairs={{0,8},{8,16},{16,24},{1,9},{9,17},{17,25},{2,10},{10,18},{18,26},{... | collective-permute-start | bytes 61448 | tf_op jit(solution)/shard_map/while/body/eval_jaxpr/ppermute | solution.py:14
  66.8 10.6 %collective-permute-start = (f32[2,1,2,5,256]{4,3,0,2,1:T(8,128)S(1)}, f32[2,1,2,5,256]{4,3,0,2,1:T(8,128)S(1)}, u32[]{:S(2)}, u32[]{:S(2)}) collective-permute-start(f32[2,1,2,5,256]{4,3,0,2,1:T(8,128)S(1)} %get-tuple-element.190), channel_id=1, source_target_pairs={{8,0},{16,8},{24,16},{9,1},{17,9},{25,17},{10,2},{18,10},{26,18},{... | collective-permute-start | bytes 61448 | tf_op jit(solution)/shard_map/while/body/eval_jaxpr/ppermute | solution.py:17
  71.4 6.0 %collective-permute-start.1 = (f32[2,1,2,5,256]{4,3,0,2,1:T(8,128)S(1)}, f32[2,1,2,5,256]{4,3,0,2,1:T(8,128)S(1)}, u32[]{:S(2)}, u32[]{:S(2)}) collective-permute-start(f32[2,1,2,5,256]{4,3,0,2,1:T(8,128)S(1)} %get-tuple-element.191), channel_id=1, source_target_pairs={{0,8},{8,16},{16,24},{1,9},{9,17},{17,25},{2,10},{10,18},{18,26},{... | collective-permute-start | bytes 61448 | tf_op jit(solution)/shard_map/while/body/eval_jaxpr/ppermute | solution.py:14
  81.7 10.6 %collective-permute-start = (f32[2,1,2,5,256]{4,3,0,2,1:T(8,128)S(1)}, f32[2,1,2,5,256]{4,3,0,2,1:T(8,128)S(1)}, u32[]{:S(2)}, u32[]{:S(2)}) collective-permute-start(f32[2,1,2,5,256]{4,3,0,2,1:T(8,128)S(1)} %get-tuple-element.190), channel_id=1, source_target_pairs={{8,0},{16,8},{24,16},{9,1},{17,9},{25,17},{10,2},{18,10},{26,18},{... | collective-permute-start | bytes 61448 | tf_op jit(solution)/shard_map/while/body/eval_jaxpr/ppermute | solution.py:17
  86.3 6.0 %collective-permute-start.1 = (f32[2,1,2,5,256]{4,3,0,2,1:T(8,128)S(1)}, f32[2,1,2,5,256]{4,3,0,2,1:T(8,128)S(1)}, u32[]{:S(2)}, u32[]{:S(2)}) collective-permute-start(f32[2,1,2,5,256]{4,3,0,2,1:T(8,128)S(1)} %get-tuple-element.191), channel_id=1, source_target_pairs={{0,8},{8,16},{16,24},{1,9},{9,17},{17,25},{2,10},{10,18},{18,26},{... | collective-permute-start | bytes 61448 | tf_op jit(solution)/shard_map/while/body/eval_jaxpr/ppermute | solution.py:14
  96.6 6.4 %collective-permute-start.2 = (f32[4,2,1,2,4,256]{5,4,1,3,2,0:T(4,128)S(1)}, f32[4,2,1,2,4,256]{5,4,1,3,2,0:T(4,128)S(1)}, u32[]{:S(2)}, u32[]{:S(2)}) collective-permute-start(f32[4,2,1,2,4,256]{5,4,1,3,2,0:T(4,128)S(1)} %get-tuple-element.147), channel_id=1, source_target_pairs={{8,0},{16,8},{24,16},{9,1},{17,9},{25,17},{10,2},{18,10},{26,18},{... | collective-permute-start | bytes 196616 | tf_op jit(solution)/shard_map/ppermute | solution.py:17
  101.3 6.2 %collective-permute-start.3 = (f32[4,2,1,2,4,256]{5,4,1,3,2,0:T(4,128)S(1)}, f32[4,2,1,2,4,256]{5,4,1,3,2,0:T(4,128)S(1)}, u32[]{:S(2)}, u32[]{:S(2)}) collective-permute-start(f32[4,2,1,2,4,256]{5,4,1,3,2,0:T(4,128)S(1)} %get-tuple-element.148), channel_id=1, source_target_pairs={{0,8},{8,16},{16,24},{1,9},{9,17},{17,25},{2,10},{10,18},{18,26},{... | collective-permute-start | bytes 196616 | tf_op jit(solution)/shard_map/ppermute | solution.py:14
  109.7 2.8 %copy-start.1 = (f32[4,1,64,256]{3,1,2,0:T(1,128)S(1)}, f32[4,1,64,256]{3,1,2,0:T(1,128)}, u32[]{:S(2)}) copy-start(f32[4,1,64,256]{3,1,2,0:T(1,128)} %stack.59) | copy-start | bytes 786436
Sparse Core Ops, SparseCore 0:
  8.9 27.4 all-gather.1
  165.2 42.0 reduce-scatter.1
where the time goes:
time: 217 us; the launch traced here: 214 us
  waiting for transfers between devices  74.3 us (34%)
  blocking collectives  47.2 us (22%)
  starting transfers between devices  28.1 us (13%)
  local copies, waits for them, and re-layouts  21.4 us (10%)
  other arithmetic  19.7 us (9%)
  between operations  14.2 us (7%)
  matrix products  8.77 us (4%)
    all_to_all x1, blocking collectives, per_device(): lax.all_to_all(row_terms, 'depth', split_axis=1, concat_axis=0, tiled=True)  47.2 us
    reduce_scatter x1, waiting for transfers between devices, per_device(): return lax.psum_scatter(terms, 'freq', scatter_dimension=0, tiled=True)  42.3 us
    all_gather x1, waiting for transfers between devices, per_device(): all_classes = lax.all_gather(classes, 'depth', axis=0, tiled=True)  26.5 us
    ppermute x5, starting transfers between devices, padded_2(): lax.ppermute(lax.slice_in_dim(block, 0, width, axis=dim), axis, backward)  21.6 us
    sub x16, other arithmetic, extrapolate(): following = 2.0 * apply_masked(current, keep) - earlier  11.7 us
    another operation x9, local copies, waits for them, and re-layouts, correlate(): stacked = jnp.stack(offsets, axis=1)  9.35 us
    dot_general x4, matrix products, march_level(): jnp.dot(all_rows, one_hot, precision=lax.Precision.HIGHEST, preferred_ele...  8.63 us
    ppermute x5, starting transfers between devices, padded_2(): lax.ppermute(lax.slice_in_dim(block, block.shape[dim] - width, None, axis...  6.46 us
  transfers between devices with their start and end apart: 12, of which 4 were waited for; matrix products, arithmetic and copies ran while one was open for 10% of the time, Pallas kernels for 0%

commit v1 on v0

v1 whole, which is shorter than its diff:
```python
import functools

import jax
import jax.numpy as jnp
from jax import lax
from jax.experimental import pallas as pl
from jax.experimental.pallas import tpu as pltpu
from jax.sharding import PartitionSpec as P

H = 8
LANES = 128
SUB = 8


def flip_rows(v, sub):
    v = pltpu.roll(v, 4, 0)
    v = jnp.where((sub & 2) == 0, pltpu.roll(v, 6, 0), pltpu.roll(v, 2, 0))
    return jnp.where((sub & 1) == 0, pltpu.roll(v, 7, 0), pltpu.roll(v, 1, 0))


def kernel(
    cfg,
    source,
    receiver,
    classes,
    tables,
    out,
    cheb,
    mirrored,
    cls,
    terms,
    pair_buf,
    ring_buf,
    done_buf,
    load_sem,
    own_cls_sem,
    cls_send,
    cls_recv,
    fwd_send,
    fwd_recv,
    pair_send,
    pair_recv,
    ring_send,
    ring_recv,
    out_send,
    out_recv,
):
    nd, nf, rows_x, cols_y, K, W = (cfg[n] for n in ("nd", "nf", "rows_x", "cols_y", "K", "W"))
    nh = cols_y // LANES
    rows_here = rows_x // nd
    half = rows_here // 2
    groups = nf // 2
    piece = rows_here // nf
    rows_out = rows_x // nf
    owners = nf // nd
    out_parts = rows_out // piece
    wide = (W - rows_here) // 2
    cls_half = W // 2
    scaling = float(nf) ** -0.5

    d = lax.axis_index("depth")
    f = lax.axis_index("freq")
    core = lax.rem(f, 2)
    chip = f // 2
    mate = f + 1 - 2 * core

    def window(depth):
        return pl.multiple_of(jnp.minimum(jnp.maximum(depth * rows_here - wide, 0), rows_x - W), SUB)

    start = window(d)
    base = pl.multiple_of(d * rows_here - start, SUB)

    def remote(src, dst, send, recv, dep, fre):
        return pltpu.make_async_remote_copy(
            src_ref=src,
            dst_ref=dst,
            send_sem=send,
            recv_sem=recv,
            device_id={"depth": dep, "freq": fre},
            device_id_type=pl.DeviceIdType.MESH,
        )

    place = core * half + chip * piece
    goal = d * owners + place // rows_out
    goal_part = lax.rem(place, rows_out) // piece
    from_depth = f // owners

    def giver(part):
        row = lax.rem(f, owners) * rows_out + part * piece
        return 2 * (lax.rem(row, half) // piece) + row // half

    def is_mine(part):
        return jnp.logical_and(from_depth == d, giver(part) == f)

    loads = []
    for comp in range(4):
        ref = source if comp < 2 else receiver
        for h in range(nh):
            loads.append(
                pltpu.make_async_copy(
                    ref.at[0, comp % 2, pl.ds(start, W), pl.ds(h * LANES, LANES)],
                    cheb.at[0, comp, h, pl.ds(SUB, W), :],
                    load_sem.at[comp * nh + h],
                )
            )
            loads[-1].start()
    own_cls = pltpu.make_async_copy(classes.at[0, pl.ds(start, W)], cls.at[d], own_cls_sem)
    own_cls.start()

    barrier = pltpu.get_barrier_semaphore()

    def greet(dep, fre):
        pl.semaphore_signal(
            barrier,
            inc=1,
            device_id={"depth": dep, "freq": fre},
            device_id_type=pl.DeviceIdType.MESH,
        )

    for s in range(1, nd):
        greet(lax.rem(d + s, nd), f)
    greet(d, mate)
    for s in range(1, groups):
        greet(d, 2 * lax.rem(chip + s, groups) + core)
    for part in range(out_parts):

        @pl.when(jnp.logical_not(is_mine(part)))
        def _():
            greet(from_depth, giver(part))

    targets = (nd - 1) + 1 + (groups - 1) + nd
    pl.semaphore_wait(barrier, targets - jnp.where(goal == f, 1, 0))

    cls_rows = pl.multiple_of(core * cls_half, SUB)
    cls_copies = []
    for s in range(1, nd):
        to = lax.rem(d + s, nd)
        src_row = pl.multiple_of(window(to) + cls_rows, SUB)
        copy = remote(
            classes.at[0, pl.ds(src_row, cls_half)],
            cls.at[d, pl.ds(cls_rows, cls_half)],
            cls_send.at[s - 1],
            cls_recv.at[d],
            to,
            f,
        )
        copy.start()
        cls_copies.append(copy)

    def forward(l):
        part = cls.at[l, pl.ds(cls_rows, cls_half)]
        return remote(part, part, fwd_send.at[l], fwd_recv.at[l], d, mate)

    def pass_on(l):
        @pl.when(d != l)
        def _():
            part = cls.at[l, pl.ds(cls_rows, cls_half)]
            remote(part, part, cls_send.at[0], cls_recv.at[l], d, mate).wait_recv()
            forward(l).start()

    def classes_ready(l):
        @pl.when(d != l)
        def _():
            forward(l).wait_recv()

        @pl.when(d == l)
        def _():
            own_cls.wait()

    zero = jnp.zeros((SUB, LANES), jnp.float32)
    for comp in range(4):
        for h in range(nh):
            for k in range(K):
                cheb[k, comp, h, 0:SUB, :] = zero
                cheb[k, comp, h, W + SUB : W + 2 * SUB, :] = zero
            if comp < 2:
                mirrored[comp, h, 0:SUB, :] = zero
                mirrored[comp, h, W + SUB : W + 2 * SUB, :] = zero

    lane = lax.broadcasted_iota(jnp.int32, (SUB, LANES), 1)
    sub = lax.broadcasted_iota(jnp.int32, (SUB, LANES), 0)
    first_lane = lane == 0
    last_lane = lane == LANES - 1

    for copy in loads:
        copy.wait()

    def chebyshev(k):
        def strip(i, carry):
            r0 = pl.multiple_of(i * SUB, SUB)
            for comp in range(4):
                twice, single, along, lefts, rights = [], [], [], [], []
                for h in range(nh):
                    v = cheb[k - 1, comp, h, pl.ds(r0 + SUB, SUB), :]
                    up = cheb[k - 1, comp, h, pl.ds(r0 + SUB - 1, SUB), :]
                    down = cheb[k - 1, comp, h, pl.ds(r0 + SUB + 1, SUB), :]
                    v2 = v + v
                    x_sum = up + down + v2
                    single.append(v)
                    twice.append(v2)
                    along.append(x_sum)
                    lefts.append(pltpu.roll(x_sum, 1, 1))
                    rights.append(pltpu.roll(x_sum, LANES - 1, 1))
                for h in range(nh):
                    left = jnp.where(first_lane, lefts[h - 1] if h > 0 else 0.0, lefts[h])
                    right = jnp.where(last_lane, rights[h + 1] if h + 1 < nh else 0.0, rights[h])
                    total = left + right + (along[h] + along[h])
                    if k == 1:
                        result = 0.125 * total - single[h]
                    else:
                        earlier = cheb[k - 2, comp, h, pl.ds(r0 + SUB, SUB), :]
                        result = 0.25 * total - (twice[h] + earlier)
                    cheb[k, comp, h, pl.ds(r0 + SUB, SUB), :] = result
            return carry

        lax.fori_loop(0, W // SUB, strip, 0)

    def combine(l):
        def strip(i, carry):
            r0 = pl.multiple_of(i * SUB, SUB)
            rows = pl.ds(r0 + SUB, SUB)
            for h in range(nh):
                which = cls[l, pl.ds(r0, SUB), h * LANES : (h + 1) * LANES]
                sums = None
                for k in range(K):
                    cr, ci = (
                        jnp.take_along_axis(
                            jnp.broadcast_to(tables[p * K + k : p * K + k + 1, :], (SUB, LANES)),
                            which,
                            axis=1,
                            mode="promise_in_bounds",
                        )
                        for p in range(2)
                    )
                    sr, si, rr, ri = (cheb[k, comp, h, rows, :] for comp in range(4))
                    new = (
                        cr * sr + ci * si,
                        cr * si - ci * sr,
                        cr * rr - ci * ri,
                        cr * ri + ci * rr,
                    )
                    sums = new if sums is None else tuple(a + b for a, b in zip(sums, new))
                for comp in range(4):
                    cheb[0, comp, h, rows, :] = sums[comp]
                for comp in range(2):
                    mirrored[comp, h, pl.ds(pl.multiple_of(W - r0, SUB), SUB), :] = flip_rows(
                        sums[comp], sub
                    )
            return carry

        lax.fori_loop(0, W // SUB, strip, 0)

    def correlate(l, first):
        def row(i, carry):
            r = first + i
            x = base + r
            for h in range(nh):
                total = None
                for part in range(2):
                    src = mirrored[part, h, pl.ds(W + 3 - x, SUB), :]
                    rec = cheb[0, 2 + part, h, pl.ds(x + 4, SUB), :]
                    total = src * rec if total is None else total + src * rec
                terms[l, r, :, h * LANES : (h + 1) * LANES] = total
            return carry

        lax.fori_loop(0, half, row, 0, unroll=4)

    def pair_copy(l):
        return remote(
            terms.at[l, pl.ds((1 - core) * half, half)],
            pair_buf.at[l],
            pair_send.at[l],
            pair_recv.at[l],
            d,
            mate,
        )

    def ring_copy(l, s):
        other = lax.rem(chip + s, groups)
        return remote(
            terms.at[l, pl.ds(core * half + other * piece, piece)],
            ring_buf.at[l, s - 1],
            ring_send.at[l, s - 1],
            ring_recv.at[l, s - 1],
            d,
            2 * other + core,
        )

    def out_copy(l):
        return remote(
            done_buf.at[l],
            out.at[pl.ds(goal_part * piece, piece), 0],
            out_send.at[l],
            out_recv.at[goal_part],
            l,
            goal,
        )

    def pair_sum(l):
        pair_copy(l).wait_recv()
        for s in list(range(1, groups)) + [0]:
            at = lax.rem(chip + s, groups) * piece
            rows = pl.ds(core * half + at, piece)
            terms[l, rows] = terms[l, rows] + pair_buf[l, pl.ds(at, piece)]
            if s > 0:
                ring_copy(l, s).start()

    def ring_sum(l):
        total = terms[l, pl.ds(place, piece)]
        for s in range(1, groups):
            ring_copy(l, s).wait_recv()
            total = total + ring_buf[l, s - 1]
        total = total * scaling
        mine = jnp.logical_and(l == d, goal == f)

        @pl.when(mine)
        def _():
            out[pl.ds(goal_part * piece, piece), 0] = total

        @pl.when(jnp.logical_not(mine))
        def _():
            done_buf[l] = total
            out_copy(l).start()

    for l in range(nd):
        for k in range(1, K):
            chebyshev(k)
        if l == 0:
            pass_on(0)
        else:
            pair_sum(l - 1)
        classes_ready(l)
        combine(l)
        if l >= 2:
            ring_sum(l - 2)
        correlate(l, (1 - core) * half)
        pair_copy(l).start()
        correlate(l, core * half)
        if l + 1 < nd:
            pass_on(l + 1)
    if nd >= 2:
        ring_sum(nd - 2)
    pair_sum(nd - 1)
    ring_sum(nd - 1)

    for copy in cls_copies:
        copy.wait_send()
    for l in range(nd):

        @pl.when(d != l)
        def _():
            forward(l).wait_send()

        pair_copy(l).wait_send()
        for s in range(1, groups):
            ring_copy(l, s).wait_send()

        @pl.when(jnp.logical_not(jnp.logical_and(l == d, goal == f)))
        def _():
            out_copy(l).wait_send()

    for part in range(out_parts):

        @pl.when(jnp.logical_not(is_mine(part)))
        def _():
            remote(
                done_buf.at[0],
                out.at[pl.ds(part * piece, piece), 0],
                out_send.at[0],
                out_recv.at[part],
                from_depth,
                giver(part),
            ).wait_recv()


def solution(mesh):
    nd, nf = mesh.shape["depth"], mesh.shape["freq"]

    def per_device(source, receiver, classes, coef_table, freq_list):
        rows_x, cols_y = source.shape[2], source.shape[3]
        class_count, K = coef_table.shape[0], coef_table.shape[3]
        rows_here = rows_x // nd
        reach = nd * (K - 1) + H // 2
        wide = -(-reach // SUB) * SUB
        W = min(rows_x, rows_here + 2 * wide)
        nh = cols_y // LANES
        groups = nf // 2
        piece = rows_here // nf
        rows_out = rows_x // nf
        cfg = dict(nd=nd, nf=nf, rows_x=rows_x, cols_y=cols_y, K=K, W=W)
        own = lax.dynamic_index_in_dim(coef_table, freq_list[0], 1, keepdims=False)
        tables = jnp.transpose(own, (1, 2, 0)).reshape(2 * K, class_count)
        tables = jnp.pad(tables, [(0, 0), (0, LANES - class_count)])
        any_space = pl.BlockSpec(memory_space=pl.ANY)
        vmem = pl.BlockSpec(memory_space=pltpu.VMEM)
        dma = pltpu.SemaphoreType.DMA
        return pl.pallas_call(
            functools.partial(kernel, cfg),
            out_shape=jax.ShapeDtypeStruct((rows_out, 1, H, cols_y), jnp.float32),
            in_specs=[any_space, any_space, any_space, vmem],
            out_specs=vmem,
            scratch_shapes=[
                pltpu.VMEM((K, 4, nh, W + 2 * SUB, LANES), jnp.float32),
                pltpu.VMEM((2, nh, W + 2 * SUB, LANES), jnp.float32),
                pltpu.VMEM((nd, W, cols_y), jnp.int32),
                pltpu.VMEM((nd, rows_here, H, cols_y), jnp.float32),
                pltpu.VMEM((nd, rows_here // 2, H, cols_y), jnp.float32),
                pltpu.VMEM((nd, max(groups - 1, 1), piece, H, cols_y), jnp.float32),
                pltpu.VMEM((nd, piece, H, cols_y), jnp.float32),
                dma((4 * nh,)),
                dma,
                dma((nd,)),
                dma((nd,)),
                dma((nd,)),
                dma((nd,)),
                dma((nd,)),
                dma((nd,)),
                dma((nd, max(groups - 1, 1))),
                dma((nd, max(groups - 1, 1))),
                dma((nd,)),
                dma((rows_out // piece,)),
            ],
            compiler_params=pltpu.CompilerParams(
                collective_id=0, has_side_effects=True, vmem_limit_bytes=32 * 1024 * 1024
            ),
        )(source, receiver, classes, tables)

    return jax.shard_map(
        per_device,
        mesh=mesh,
        in_specs=(
            P("freq", None, None, None),
            P("freq", None, None, None),
            P("depth", None, None),
            P(),
            P("freq"),
        ),
        out_specs=P("freq", "depth", None, None),
        check_vma=False,
    )
```

time: 217 us -> 59.6 us (0.27); the launches traced: 214 us -> 59.3 us
  waiting for transfers between devices: 74.3 us -> 0 us
  Pallas kernels: 0 us -> 54.7 us
  blocking collectives: 47.2 us -> 0 us
  starting transfers between devices: 28.1 us -> 0 us
  other arithmetic: 19.7 us -> 0 us
  local copies, waits for them, and re-layouts: 21.4 us -> 3.91 us
  between operations: 14.2 us -> 0.68 us
  matrix products: 8.77 us -> 0 us
    pallas_call x0 -> x1, Pallas kernels: none -> 54.7 us  [per_device(): pl.pallas_call(functools.partial(kernel, cfg), out_shape=jax.ShapeDtypeSt...]
    all_to_all x1 -> x0, blocking collectives: 47.2 us -> none  [per_device(): lax.all_to_all(row_terms, 'depth', split_axis=1, concat_axis=0, tiled=True)]
    reduce_scatter x1 -> x0, waiting for transfers between devices: 42.3 us -> none  [per_device(): return lax.psum_scatter(terms, 'freq', scatter_dimension=0, tiled=True)]
    ppermute x10 -> x0, starting transfers between devices: 28.1 us -> none  [the longest x5 21.6 us: padded_2(): lax.ppermute(lax.slice_in_dim(block, 0, width, axis=dim), axis, backward)]
    all_gather x1 -> x0, waiting for transfers between devices: 26.5 us -> none  [per_device(): all_classes = lax.all_gather(classes, 'depth', axis=0, tiled=True)]
    sub x20 -> x0, other arithmetic: 13 us -> none  [the longest x16 11.7 us: extrapolate(): following = 2.0 * apply_masked(current, keep) - earlier]
    another operation x9 -> x0, local copies, waits for them, and re-layouts: 9.35 us -> none  [correlate(): stacked = jnp.stack(offsets, axis=1)]
    dot_general x5 -> x0, matrix products: 8.77 us -> none  [the longest x4 8.63 us: march_level(): jnp.dot(all_rows, one_hot, precision=lax.Precision.HIGHEST, preferred_ele...]
  transfers between devices with their start and end apart: 12 -> 0, of which waited for: 4 -> 0; matrix products, arithmetic and copies ran while one was open for 10% -> 0% of each run, Pallas kernels for 0% -> 0%
where the time goes in v1:
time: 59.6 us; the launch traced here: 59.3 us
  Pallas kernels  54.7 us (92%)
  local copies, waits for them, and re-layouts  3.91 us (7%)
  between operations  0.68 us (1%)
    pallas_call x1, Pallas kernels, per_device(): pl.pallas_call(functools.partial(kernel, cfg), out_shape=jax.ShapeDtypeSt...  54.7 us
    unnamed x9, local copies, waits for them, and re-layouts  3.89 us

profile of v1, /device:TPU:26, one launch (start us, length us, event | category | flops | bytes accessed | tf_op | source)
XLA Modules:
  0.0 59.3 jit_solution(17151280595620896861)
XLA Ops:
  0.0 0.0 copy-start
  0.7 0.1 copy-done
  0.8 0.0 copy-start.1
  0.8 1.0 %copy-done.1 = f32[1,2,256,256]{3,2,1,0:T(8,128)S(1)} copy-done((f32[1,2,256,256]{3,2,1,0:T(8,128)S(1)}, f32[1,2,256,256]{3,2,1,0:T(8,128)}, u32[]{:S(2)}) %copy-start.1) | copy-done | bytes 524312
  1.9 0.0 copy-start.2
  1.9 1.0 %copy-done.2 = f32[1,2,256,256]{3,2,1,0:T(8,128)S(1)} copy-done((f32[1,2,256,256]{3,2,1,0:T(8,128)S(1)}, f32[1,2,256,256]{3,2,1,0:T(8,128)}, u32[]{:S(2)}) %copy-start.2) | copy-done | bytes 524312
  2.9 0.0 copy-start.3
  2.9 0.9 %copy-done.3 = s32[1,256,256]{2,1,0:T(8,128)S(1)} copy-done((s32[1,256,256]{2,1,0:T(8,128)S(1)}, s32[1,256,256]{2,1,0:T(8,128)}, u32[]{:S(2)}) %copy-start.3) | copy-done | bytes 262168
  3.9 54.7 %shard_map.55 = f32[32,1,8,256]{3,2,1,0:T(8,128)S(1)} custom-call(f32[1,2,256,256]{3,2,1,0:T(8,128)S(1)} %copy-done.1, f32[1,2,256,256]{3,2,1,0:T(8,128)S(1)} %copy-done.2, s32[1,256,256]{2,1,0:T(8,128)S(1)} %copy-done.3, f32[12,128]{1,0:T(8,128)S(1)} %pad.4.tables), custom_call_target="tpu_custom_call" | custom-call | tf_op jit(solution)/shard_map/pallas_call | solution.py:397
  58.6 0.7 %copy.9 = f32[32,1,8,256]{3,2,1,0:T(8,128)} copy(f32[32,1,8,256]{3,2,1,0:T(8,128)S(1)} %shard_map.55) | data formatting | bytes 524288
  (4 shorter events, 0.0 us)
Async XLA Ops:
  0.0 0.8 %copy-start = (f32[16,8,2,6]{0,2,3,1:T(2,128)S(1)}, f32[16,8,2,6]{0,2,3,1:T(2,128)}, u32[]{:S(2)}) copy-start(f32[16,8,2,6]{0,2,3,1:T(2,128)} %param.8) | copy-start | bytes 18436
  0.8 1.0 %copy-start.1 = (f32[1,2,256,256]{3,2,1,0:T(8,128)S(1)}, f32[1,2,256,256]{3,2,1,0:T(8,128)}, u32[]{:S(2)}) copy-start(f32[1,2,256,256]{3,2,1,0:T(8,128)} %source.1) | copy-start | bytes 1572868
  1.9 1.0 %copy-start.2 = (f32[1,2,256,256]{3,2,1,0:T(8,128)S(1)}, f32[1,2,256,256]{3,2,1,0:T(8,128)}, u32[]{:S(2)}) copy-start(f32[1,2,256,256]{3,2,1,0:T(8,128)} %receiver.1) | copy-start | bytes 1572868
  2.9 0.9 %copy-start.3 = (s32[1,256,256]{2,1,0:T(8,128)S(1)}, s32[1,256,256]{2,1,0:T(8,128)}, u32[]{:S(2)}) copy-start(s32[1,256,256]{2,1,0:T(8,128)} %classes.1) | copy-start | bytes 786436
